TPU v7x, 32 devices: a whole 2x2x4 slice. The times are simulated.
32 devices in a mesh: seq: 4 (over z), pair: 4 (over y, core), dp: 2 (over x).
Axes of the slice: x: 2, y: 2, z: 4, core: 2. Of those that a mesh axis runs over, the one named last changes fastest.
Arguments:
- embed: bfloat16 [2048, 1536], P(('dp', 'seq')), parts along dimension 0, may hold values from -6 to 6
- attn_gain: float32 [1536], replicated, may hold values from 0.5 to 1.5
- w_query: bfloat16 [1536, 1024], P(None, 'pair'), may hold values from -2.5643096 to 2.5643096
- w_key: bfloat16 [1536, 128], replicated, may hold values from -0.104613624 to 0.104613624
- w_value: bfloat16 [1536, 128], replicated, may hold values from -0.15625 to 0.15625
- w_out: bfloat16 [1024, 1536], P('pair'), may hold values from -0.1875 to 0.1875
- pair_map: bfloat16 [128, 64, 128], P(('dp', 'seq'), 'pair'), parts along dimension 0, may hold values from -6 to 6
- w_row: bfloat16 [1536, 128], replicated, may hold values from -0.625 to 0.625
- w_col: bfloat16 [1536, 128], replicated, may hold values from -0.625 to 0.625
- pair_gain: float32 [128], replicated, may hold values from 0.5 to 1.5
- conv_weight: bfloat16 [3, 3, 128, 128], replicated, may hold values from -0.1875 to 0.1875
Outputs:
- block_out: bfloat16 [2048, 1536], P(('dp', 'seq'), 'pair'), parts along dimension 0
- new_pair: bfloat16 [128, 64, 128], P(('dp', 'seq'), 'pair'), parts along dimension 0
There are 2 independent parts, one for each index of `dp`. A program takes and returns all parts, laid end to end along the dimension named above; an argument that names none is the same for every part. Nothing has to cross between parts.
All inputs are finite; a program needn't handle non-finite values.
Results may differ from a plain program's by a relative error of at most 0.014.
Values may be sent and summed in bfloat16 or wider, within the bound.
A program may use at most 64 MiB of HBM per device.

v0:
```python
import math
import jax
import jax.numpy as jnp
from jax import lax
from jax.sharding import PartitionSpec as P

POOL = 16


def padded_2(block, sides, width):
    for axis, dim in sides:
        count = lax.axis_size(axis)
        forward = [(i, i + 1) for i in range(count - 1)]
        backward = [(target, source) for source, target in forward]
        low = lax.ppermute(
            lax.slice_in_dim(block, block.shape[dim] - width, None, axis=dim), axis, forward
        )
        high = lax.ppermute(lax.slice_in_dim(block, 0, width, axis=dim), axis, backward)
        block = jnp.concatenate([low, block, high], axis=dim)
    return block


def rms_scale(values, gain):
    return values * lax.rsqrt(jnp.mean(values * values, axis=-1, keepdims=True) + 1e-05) * gain


def rotate(tensor, positions):
    half = tensor.shape[-1] // 2
    freq = 10000.0 ** (-jnp.arange(half, dtype=jnp.float32) / half)
    angles = positions[:, None] * freq[None, :]
    cosine = jnp.cos(angles)[:, None, :]
    sine = jnp.sin(angles)[:, None, :]
    first = tensor[..., :half]
    second = tensor[..., half:]
    return jnp.concatenate(
        [first * cosine - second * sine, first * sine + second * cosine], axis=-1
    )


def per_device(
    embed, attn_gain, w_query, w_key, w_value, w_out, pair_map, w_row, w_col, pair_gain, conv_weight
):
    tokens = embed.shape[0]
    head_size = w_key.shape[1]
    local_heads = w_query.shape[1] // head_size
    normed = rms_scale(embed.astype(jnp.float32), attn_gain).astype(jnp.bfloat16)
    positions = (lax.axis_index("seq") * tokens + jnp.arange(tokens)).astype(jnp.float32)
    query = jnp.dot(normed, w_query, preferred_element_type=jnp.float32).reshape(
        tokens, local_heads, head_size
    )
    query = rotate(query, positions).transpose(1, 0, 2).astype(jnp.bfloat16)
    key = jnp.dot(normed, w_key, preferred_element_type=jnp.float32)[:, None, :]
    key = rotate(key, positions)[:, 0, :].astype(jnp.bfloat16)
    value = jnp.dot(normed, w_value, preferred_element_type=jnp.float32).astype(jnp.bfloat16)
    scale = 1.0 / head_size**0.5

    def attend_block(carry, block):
        running_max, running_sum, running_acc = carry
        key_block, value_block = block
        scores = (
            jnp.einsum("hqd,kd->hqk", query, key_block, preferred_element_type=jnp.float32) * scale
        )
        new_max = jnp.maximum(running_max, jnp.max(scores, axis=-1))
        factor = jnp.exp(running_max - new_max)
        terms = jnp.exp(scores - new_max[..., None])
        new_sum = running_sum * factor + jnp.sum(terms, axis=-1)
        mixed = jnp.einsum(
            "hqk,kd->hqd",
            terms.astype(jnp.bfloat16),
            value_block,
            preferred_element_type=jnp.float32,
        )
        return ((new_max, new_sum, running_acc * factor[..., None] + mixed), None)

    initial = (
        jnp.full((local_heads, tokens), -1e30, jnp.float32),
        jnp.zeros((local_heads, tokens), jnp.float32),
        jnp.zeros((local_heads, tokens, head_size), jnp.float32),
    )
    key_piece = lax.all_gather(key, "seq", axis=0, tiled=True)
    value_piece = lax.all_gather(value, "seq", axis=0, tiled=True)
    length = key_piece.shape[0]
    block = math.gcd(length, 1024)
    key_blocks = key_piece.reshape(length // block, block, head_size)
    value_blocks = value_piece.reshape(length // block, block, head_size)
    result, unused = lax.scan(attend_block, initial, (key_blocks, value_blocks))
    final_max, final_sum, final_acc = result
    attended = (final_acc / final_sum[..., None]).astype(jnp.bfloat16)
    attended = attended.transpose(1, 0, 2).reshape(tokens, local_heads * head_size)
    head_terms = jnp.dot(attended, w_out, preferred_element_type=jnp.float32)
    summed = lax.psum_scatter(
        head_terms.astype(jnp.bfloat16), "pair", scatter_dimension=1, tiled=True
    ).astype(jnp.float32)
    feature_count = summed.shape[1]
    residual = lax.dynamic_slice_in_dim(
        embed, lax.axis_index("pair") * feature_count, feature_count, 1
    )
    block_out = (residual.astype(jnp.float32) + summed).astype(jnp.bfloat16)
    model_width = normed.shape[1]
    pooled = jnp.mean(
        normed.astype(jnp.float32).reshape(tokens // POOL, POOL, model_width), axis=1
    ).astype(jnp.bfloat16)
    row_feat = jnp.dot(pooled, w_row, preferred_element_type=jnp.float32).astype(jnp.bfloat16)
    col_feat = jnp.dot(pooled, w_col, preferred_element_type=jnp.float32).astype(jnp.bfloat16)
    all_cols = lax.all_gather(col_feat, "seq", axis=0, tiled=True)
    column_count = pair_map.shape[1]
    my_cols = lax.dynamic_slice_in_dim(
        all_cols, lax.axis_index("pair") * column_count, column_count, 0
    )
    updated = (
        pair_map.astype(jnp.float32)
        + row_feat.astype(jnp.float32)[:, None, :] * my_cols.astype(jnp.float32)[None, :, :]
    )
    pair_normed = rms_scale(updated, pair_gain).astype(jnp.bfloat16)
    padded = padded_2(pair_normed, (("seq", 0), ("pair", 1)), 1)
    row_count = pair_map.shape[0]
    channel_count = pair_map.shape[2]
    convolved = jnp.zeros((row_count * column_count, channel_count), jnp.float32)
    for offset_row in range(3):
        for offset_col in range(3):
            window = padded[
                offset_row : offset_row + row_count, offset_col : offset_col + column_count, :
            ]
            convolved = convolved + jnp.dot(
                window.reshape(row_count * column_count, channel_count),
                conv_weight[offset_row, offset_col],
                preferred_element_type=jnp.float32,
            )
    new_pair = (updated + convolved.reshape(row_count, column_count, channel_count)).astype(
        jnp.bfloat16
    )
    return (block_out, new_pair)


def solution(mesh):
    placed = (
        P(("dp", "seq"), None),
        P(),
        P(None, "pair"),
        P(),
        P(),
        P("pair", None),
        P(("dp", "seq"), "pair", None),
        P(),
        P(),
        P(),
        P(),
    )
    return jax.shard_map(
        per_device,
        mesh=mesh,
        in_specs=placed,
        out_specs=(P(("dp", "seq"), "pair"), P(("dp", "seq"), "pair", None)),
        check_vma=False,
    )
```

profile of v0, /device:TPU:0, one launch (start us, length us, event | category | flops | bytes accessed | tf_op | source)
XLA Modules:
  0.0 97.6 jit_solution(4122709407723177928)
XLA Ops:
  7.3 1.5 %fusion.2 = f32[256]{0:T(256)S(1)} fusion(bf16[256,1536]{1,0:T(8,128)(2,1)} %param.11), kind=kLoop, calls=%fused_computation.7 | loop fusion | flops 1179392 | bytes 787456 | tf_op jit(solution)/shard_map/reduce_sum | solution.py:24
  8.8 1.7 %convert_reduce_fusion = f32[16,1536]{1,0:T(8,128)S(1)} fusion(f32[1536]{0:T(1024)} %param.12, f32[256]{0:T(256)S(1)} %add_rsqrt_fusion.1, bf16[256,1536]{1,0:T(8,128)(2,1)} %param.11), kind=kLoop, calls=%fused_computation.10 | loop fusion | flops 2334720 | bytes 891904 | tf_op jit(solution)/shard_map/reduce_sum | solution.py:100
  10.7 14.8 %all_gather.11 = bf16[64,128]{1,0:T(8,128)(2,1)S(1)} all-gather(bf16[16,128]{1,0:T(8,128)(2,1)S(1)} %convolution_convert_fusion.2), channel_id=1, replica_groups=mesh['seq'=4,'pair'=4,'dp'=2] {'seq'}, dimensions={0}, use_global_device_ids=true | all-gather | bytes 20480 | tf_op jit(solution)/shard_map/all_gather | solution.py:105
  25.9 1.3 %collective-permute-start.1 = (bf16[1,16,128]{2,1,0:T(8,128)(2,1)S(1)}, bf16[1,16,128]{2,1,0:T(8,128)(2,1)S(1)}, u32[]{:S(2)}, u32[]{:S(2)}) collective-permute-start(bf16[1,16,128]{2,1,0:T(8,128)(2,1)S(1)} %get-tuple-element.42), channel_id=1, source_target_pairs={{8,0},{16,8},{24,16},{9,1},{17,9},{25,17},{10,2},{18,10},{26,18},{... | collective-permute-start | bytes 12296 | tf_op jit(solution)/shard_map/ppermute | solution.py:18
  27.2 4.5 %collective-permute-start = (bf16[1,16,128]{2,1,0:T(8,128)(2,1)S(1)}, bf16[1,16,128]{2,1,0:T(8,128)(2,1)S(1)}, u32[]{:S(2)}, u32[]{:S(2)}) collective-permute-start(bf16[1,16,128]{2,1,0:T(8,128)(2,1)S(1)} %get-tuple-element.41), channel_id=1, source_target_pairs={{0,8},{8,16},{16,24},{1,9},{9,17},{17,25},{2,10},{10,18},{18,26},{... | collective-permute-start | bytes 12296 | tf_op jit(solution)/shard_map/ppermute | solution.py:15
  31.8 0.5 convolution_bitcast_fusion.1
  32.3 0.5 multiply_cosine_fusion
  33.2 13.8 %all-gather = bf16[1024,1,128]{0,2,1:T(8,128)(2,1)S(1)} all-gather(bf16[256,1,128]{0,2,1:T(8,128)(2,1)S(1)} %pad_maximum_fusion.3), channel_id=2, replica_groups=mesh['seq'=4,'pair'=4,'dp'=2] {'seq'}, dimensions={0}, use_global_device_ids=true | all-gather | bytes 327680 | tf_op jit(solution)/shard_map/all_gather | solution.py:80
  47.0 0.6 fusion.52
  48.0 0.6 multiply_reduce_fusion
  48.6 0.4 copy-done.10
  49.0 0.5 convolution_convert_fusion.1
  49.5 13.8 %all_gather.10 = bf16[1024,128]{0,1:T(8,128)(2,1)S(1)} all-gather(bf16[256,128]{0,1:T(8,128)(2,1)S(1)} %convolution_convert_fusion.1), channel_id=1, replica_groups=mesh['seq'=4,'pair'=4,'dp'=2] {'seq'}, dimensions={0}, use_global_device_ids=true | all-gather | bytes 327680 | tf_op jit(solution)/shard_map/all_gather | solution.py:81
  63.2 0.5 fusion
  63.8 0.6 fusion.7
  64.4 0.4 convolution_convert_fusion
  64.8 1.2 %copy.21 = bf16[256,1536]{0,1:T(8,128)(2,1)} copy(bf16[256,1536]{1,0:T(8,128)(2,1)S(1)} %convolution_convert_fusion) | data formatting | bytes 1572864
  66.1 1.3 %collective-permute-start.2 = (bf16[18,1,128]{2,1,0:T(2,128)(2,1)S(1)}, bf16[18,1,128]{2,1,0:T(2,128)(2,1)S(1)}, u32[]{:S(2)}, u32[]{:S(2)}) collective-permute-start(bf16[18,1,128]{2,1,0:T(2,128)(2,1)S(1)} %get-tuple-element.37), channel_id=1, source_target_pairs={{0,2},{2,4},{4,6},{1,3},{3,5},{5,7},{8,10},{10,12},{12,14},{9,11},... | collective-permute-start | bytes 13832 | tf_op jit(solution)/shard_map/ppermute | solution.py:15
  67.4 1.3 %collective-permute-start.3 = (bf16[18,1,128]{2,1,0:T(2,128)(2,1)S(1)}, bf16[18,1,128]{2,1,0:T(2,128)(2,1)S(1)}, u32[]{:S(2)}, u32[]{:S(2)}) collective-permute-start(bf16[18,1,128]{2,1,0:T(2,128)(2,1)S(1)} %get-tuple-element.38), channel_id=1, source_target_pairs={{2,0},{4,2},{6,4},{3,1},{5,3},{7,5},{10,8},{12,10},{14,12},{11,9},... | collective-permute-start | bytes 13832 | tf_op jit(solution)/shard_map/ppermute | solution.py:18
  68.8 3.3 %collective-permute-done.3 = bf16[18,1,128]{2,1,0:T(2,128)(2,1)S(1)} collective-permute-done((bf16[18,1,128]{2,1,0:T(2,128)(2,1)S(1)}, bf16[18,1,128]{2,1,0:T(2,128)(2,1)S(1)}, u32[]{:S(2)}, u32[]{:S(2)}) %collective-permute-start.3) | collective-permute-done | bytes 4640 | tf_op jit(solution)/shard_map/ppermute | solution.py:18
  73.5 0.7 add_convert_fusion.2
  74.2 14.7 %reduce-scatter.4.cloned.1.call-done = bf16[384,256]{1,0:T(8,128)(2,1)} async-done(((bf16[1536,256]{1,0:T(8,128)(2,1)}), bf16[384,256]{1,0:T(8,128)(2,1)}) %reduce-scatter.4.cloned.1.call-update) | async-done | bytes 196624
  88.9 1.1 %copy.22 = bf16[256,384]{1,0:T(8,128)(2,1)S(1)} copy(bf16[256,384]{0,1:T(8,128)(2,1)} %bitcast.103) | data formatting | bytes 393216
  90.0 0.7 add_convert_fusion
  (57 shorter events, 2.8 us)
Async XLA Ops:
  7.2 57.2 %copy-start = (bf16[256,1536]{1,0:T(8,128)(2,1)S(1)}, bf16[256,1536]{1,0:T(8,128)(2,1)}, u32[]{:S(2)}) copy-start(bf16[256,1536]{1,0:T(8,128)(2,1)} %param.16) | copy-start | bytes 2359300
  7.2 24.6 %copy-start.1 = (bf16[256,1536]{1,0:T(8,128)(2,1)S(1)}, bf16[256,1536]{1,0:T(8,128)(2,1)}, u32[]{:S(2)}) copy-start(bf16[256,1536]{1,0:T(8,128)(2,1)} %param.11) | copy-start | bytes 2359300
  7.2 24.6 %copy-start.6 = (f32[1536]{0:T(1024)S(1)}, f32[1536]{0:T(1024)}, u32[]{:S(2)}) copy-start(f32[1536]{0:T(1024)} %param.12) | copy-start | bytes 18436
  7.2 3.3 %copy-start.4 = (bf16[1536,128]{1,0:T(8,128)(2,1)S(1)}, bf16[1536,128]{1,0:T(8,128)(2,1)}, u32[]{:S(2)}) copy-start(bf16[1536,128]{1,0:T(8,128)(2,1)} %param.19) | copy-start | bytes 1179652
  7.2 18.3 %copy-start.3 = (bf16[1536,128]{1,0:T(8,128)(2,1)S(1)}, bf16[1536,128]{1,0:T(8,128)(2,1)}, u32[]{:S(2)}) copy-start(bf16[1536,128]{1,0:T(8,128)(2,1)} %param.18) | copy-start | bytes 1179652
  7.2 18.4 %copy-start.2 = (bf16[16,16,128]{2,1,0:T(8,128)(2,1)S(1)}, bf16[16,16,128]{2,1,0:T(8,128)(2,1)}, u32[]{:S(2)}) copy-start(bf16[16,16,128]{2,1,0:T(8,128)(2,1)} %param.17) | copy-start | bytes 196612
  7.2 18.6 %copy-start.7 = (f32[128]{0:T(128)S(1)}, f32[128]{0:T(128)}, u32[]{:S(2)}) copy-start(f32[128]{0:T(128)} %param.20) | copy-start | bytes 1540
  7.2 24.6 %copy-start.9 = (bf16[1536,128]{1,0:T(8,128)(2,1)S(1)}, bf16[1536,128]{1,0:T(8,128)(2,1)}, u32[]{:S(2)}) copy-start(bf16[1536,128]{1,0:T(8,128)(2,1)} %param.14) | copy-start | bytes 1179652
  7.3 81.7 %reduce-scatter.4.cloned.1.call-start = ((), (), s32[]{:S(2)}) async-start(), calls=%async_computation.1 | async-start | bytes 983040
  25.5 21.5 %copy-start.8 = (bf16[1536,256]{1,0:T(8,128)(2,1)S(1)}, bf16[1536,256]{1,0:T(8,128)(2,1)}, u32[]{:S(2)}) copy-start(bf16[1536,256]{1,0:T(8,128)(2,1)} %param.13) | copy-start | bytes 2359300
  25.9 40.1 %collective-permute-start.1 = (bf16[1,16,128]{2,1,0:T(8,128)(2,1)S(1)}, bf16[1,16,128]{2,1,0:T(8,128)(2,1)S(1)}, u32[]{:S(2)}, u32[]{:S(2)}) collective-permute-start(bf16[1,16,128]{2,1,0:T(8,128)(2,1)S(1)} %get-tuple-element.42), channel_id=1, source_target_pairs={{8,0},{16,8},{24,16},{9,1},{17,9},{25,17},{10,2},{18,10},{26,18},{... | collective-permute-start | bytes 12296 | tf_op jit(solution)/shard_map/ppermute | solution.py:18
  27.2 38.8 %collective-permute-start = (bf16[1,16,128]{2,1,0:T(8,128)(2,1)S(1)}, bf16[1,16,128]{2,1,0:T(8,128)(2,1)S(1)}, u32[]{:S(2)}, u32[]{:S(2)}) collective-permute-start(bf16[1,16,128]{2,1,0:T(8,128)(2,1)S(1)} %get-tuple-element.41), channel_id=1, source_target_pairs={{0,8},{8,16},{16,24},{1,9},{9,17},{17,25},{2,10},{10,18},{18,26},{... | collective-permute-start | bytes 12296 | tf_op jit(solution)/shard_map/ppermute | solution.py:15
  48.0 1.0 %copy-start.10 = (bf16[1536,128]{1,0:T(8,128)(2,1)S(1)}, bf16[1536,128]{1,0:T(8,128)(2,1)}, u32[]{:S(2)}) copy-start(bf16[1536,128]{1,0:T(8,128)(2,1)} %param.15) | copy-start | bytes 1179652
  64.8 3.9 %copy-start.5 = (bf16[3,3,128,128]{3,2,1,0:T(8,128)(2,1)S(1)}, bf16[3,3,128,128]{3,2,1,0:T(8,128)(2,1)}, u32[]{:S(2)}) copy-start(bf16[3,3,128,128]{3,2,1,0:T(8,128)(2,1)} %param.21) | copy-start | bytes 884740
  66.1 2.8 %collective-permute-start.2 = (bf16[18,1,128]{2,1,0:T(2,128)(2,1)S(1)}, bf16[18,1,128]{2,1,0:T(2,128)(2,1)S(1)}, u32[]{:S(2)}, u32[]{:S(2)}) collective-permute-start(bf16[18,1,128]{2,1,0:T(2,128)(2,1)S(1)} %get-tuple-element.37), channel_id=1, source_target_pairs={{0,2},{2,4},{4,6},{1,3},{3,5},{5,7},{8,10},{10,12},{12,14},{9,11},... | collective-permute-start | bytes 13832 | tf_op jit(solution)/shard_map/ppermute | solution.py:15
  67.4 4.8 %collective-permute-start.3 = (bf16[18,1,128]{2,1,0:T(2,128)(2,1)S(1)}, bf16[18,1,128]{2,1,0:T(2,128)(2,1)S(1)}, u32[]{:S(2)}, u32[]{:S(2)}) collective-permute-start(bf16[18,1,128]{2,1,0:T(2,128)(2,1)S(1)} %get-tuple-element.38), channel_id=1, source_target_pairs={{2,0},{4,2},{6,4},{3,1},{5,3},{7,5},{10,8},{12,10},{14,12},{11,9},... | collective-permute-start | bytes 13832 | tf_op jit(solution)/shard_map/ppermute | solution.py:18
Sparse Core Ops, SparseCore 0:
  66.1 22.7 reduce-scatter.3
where the time goes:
time: 97.9 us; the launch traced here: 97.6 us
  blocking collectives  42.4 us (43%)
  waiting for transfers between devices  18.1 us (18%)
  between operations  14.5 us (15%)
  starting transfers between devices  8.46 us (9%)
  other arithmetic  6.37 us (7%)
  matrix products  4.75 us (5%)
  local copies, waits for them, and re-layouts  3.04 us (3%)
    all_gather x1, blocking collectives, per_device(): all_cols = lax.all_gather(col_feat, 'seq', axis=0, tiled=True)  14.8 us
    unnamed x2, waiting for transfers between devices  14.8 us
    all_gather x1, blocking collectives, per_device(): key_piece = lax.all_gather(key, 'seq', axis=0, tiled=True)  13.8 us
    all_gather x1, blocking collectives, per_device(): value_piece = lax.all_gather(value, 'seq', axis=0, tiled=True)  13.8 us
    ppermute x2, starting transfers between devices, padded_2(): lax.ppermute(lax.slice_in_dim(block, block.shape[dim] - width, None, axis...  5.84 us
    ppermute x2, waiting for transfers between devices, padded_2(): lax.ppermute(lax.slice_in_dim(block, 0, width, axis=dim), axis, backward)  3.34 us
    unnamed x26, local copies, waits for them, and re-layouts  2.96 us
    ppermute x2, starting transfers between devices, padded_2(): lax.ppermute(lax.slice_in_dim(block, 0, width, axis=dim), axis, backward)  2.58 us
  transfers between devices with their start and end apart: 5, of which 2 were waited for; matrix products, arithmetic and copies ran while one was open for 8% of the time, Pallas kernels for 0%

commit v1 on v0

--- a/solution.py
+++ b/solution.py
@@ -77,8 +77,11 @@
         jnp.zeros((local_heads, tokens), jnp.float32),
         jnp.zeros((local_heads, tokens, head_size), jnp.float32),
     )
-    key_piece = lax.all_gather(key, "seq", axis=0, tiled=True)
-    value_piece = lax.all_gather(value, "seq", axis=0, tiled=True)
+    key_piece, value_piece = jnp.split(
+        lax.all_gather(jnp.concatenate([key, value], axis=1), "seq", axis=0, tiled=True),
+        [key.shape[1]],
+        axis=1,
+    )
     length = key_piece.shape[0]
     block = math.gcd(length, 1024)
     key_blocks = key_piece.reshape(length // block, block, head_size)

time: 97.9 us -> 85.9 us (0.88)
  blocking collectives: 42.4 us -> 29.6 us
  matrix products: 4.75 us -> 5.89 us
    all_gather x2 -> x1, blocking collectives: 27.6 us -> 14.8 us  [per_device(): lax.all_gather(jnp.concatenate([key, value], axis=1), 'seq', axis=0, tile...]
    dot_general x1, matrix products: 0.58 us -> 1.7 us  [per_device(): jnp.dot(normed, w_query, preferred_element_type=jnp.float32)]
    unnamed x26 -> x24, local copies, waits for them, and re-layouts: 2.96 us -> 2.54 us
  transfers between devices with their start and end apart: 5 -> 5, of which waited for: 2 -> 2; matrix products, arithmetic and copies ran while one was open for 8% -> 11% of each run, Pallas kernels for 0% -> 0%
where the time goes in v1:
time: 85.9 us; the launch traced here: 85.6 us
  blocking collectives  29.6 us (34%)
  waiting for transfers between devices  18.2 us (21%)
  between operations  14.5 us (17%)
  starting transfers between devices  8.46 us (10%)
  other arithmetic  6.39 us (7%)
  matrix products  5.89 us (7%)
  local copies, waits for them, and re-layouts  2.62 us (3%)
    unnamed x2, waiting for transfers between devices  14.8 us
    all_gather x1, blocking collectives, per_device(): lax.all_gather(jnp.concatenate([key, value], axis=1), 'seq', axis=0, tile...  14.8 us
    all_gather x1, blocking collectives, per_device(): all_cols = lax.all_gather(col_feat, 'seq', axis=0, tiled=True)  14.8 us
    ppermute x2, starting transfers between devices, padded_2(): lax.ppermute(lax.slice_in_dim(block, block.shape[dim] - width, None, axis...  5.84 us
    ppermute x2, waiting for transfers between devices, padded_2(): lax.ppermute(lax.slice_in_dim(block, 0, width, axis=dim), axis, backward)  3.33 us
    ppermute x2, starting transfers between devices, padded_2(): lax.ppermute(lax.slice_in_dim(block, 0, width, axis=dim), axis, backward)  2.58 us
    unnamed x24, local copies, waits for them, and re-layouts  2.54 us
  transfers between devices with their start and end apart: 5, of which 2 were waited for; matrix products, arithmetic and copies ran while one was open for 11% of the time, Pallas kernels for 0%

profile of v1, /device:TPU:0, one launch (start us, length us, event | category | flops | bytes accessed | tf_op | source)
XLA Modules:
  0.0 85.6 jit_solution(437592519216459517)
XLA Ops:
  7.3 1.5 %fusion.2 = f32[256]{0:T(256)S(1)} fusion(bf16[256,1536]{1,0:T(8,128)(2,1)} %param.11), kind=kLoop, calls=%fused_computation.7 | loop fusion | flops 1179392 | bytes 787456 | tf_op jit(solution)/shard_map/reduce_sum | solution.py:24
  8.8 1.7 %convert_reduce_fusion = f32[16,1536]{1,0:T(8,128)S(1)} fusion(f32[1536]{0:T(1024)} %param.12, f32[256]{0:T(256)S(1)} %add_rsqrt_fusion.1, bf16[256,1536]{1,0:T(8,128)(2,1)} %param.11), kind=kLoop, calls=%fused_computation.10 | loop fusion | flops 2334720 | bytes 891904 | tf_op jit(solution)/shard_map/reduce_sum | solution.py:103
  10.7 14.8 %all_gather.7 = bf16[64,128]{1,0:T(8,128)(2,1)S(1)} all-gather(bf16[16,128]{1,0:T(8,128)(2,1)S(1)} %convolution_convert_fusion.2), channel_id=1, replica_groups=mesh['seq'=4,'pair'=4,'dp'=2] {'seq'}, dimensions={0}, use_global_device_ids=true | all-gather | bytes 20480 | tf_op jit(solution)/shard_map/all_gather | solution.py:108
  25.5 0.2 fusion.9
  25.9 1.3 %collective-permute-start.1 = (bf16[1,16,128]{2,1,0:T(8,128)(2,1)S(1)}, bf16[1,16,128]{2,1,0:T(8,128)(2,1)S(1)}, u32[]{:S(2)}, u32[]{:S(2)}) collective-permute-start(bf16[1,16,128]{2,1,0:T(8,128)(2,1)S(1)} %get-tuple-element.42), channel_id=1, source_target_pairs={{8,0},{16,8},{24,16},{9,1},{17,9},{25,17},{10,2},{18,10},{26,18},{... | collective-permute-start | bytes 12296 | tf_op jit(solution)/shard_map/ppermute | solution.py:18
  27.2 4.5 %collective-permute-start = (bf16[1,16,128]{2,1,0:T(8,128)(2,1)S(1)}, bf16[1,16,128]{2,1,0:T(8,128)(2,1)S(1)}, u32[]{:S(2)}, u32[]{:S(2)}) collective-permute-start(bf16[1,16,128]{2,1,0:T(8,128)(2,1)S(1)} %get-tuple-element.41), channel_id=1, source_target_pairs={{0,8},{8,16},{16,24},{1,9},{9,17},{17,25},{2,10},{10,18},{18,26},{... | collective-permute-start | bytes 12296 | tf_op jit(solution)/shard_map/ppermute | solution.py:15
  31.8 0.5 convolution_convert_fusion.1
  32.3 0.5 convolution_bitcast_fusion.1
  32.8 0.5 multiply_cosine_fusion
  33.4 0.3 fusion.21
  33.7 14.8 %all_gather.6 = bf16[1024,256]{0,1:T(8,128)(2,1)S(1)} all-gather(bf16[256,256]{0,1:T(8,128)(2,1)S(1)} %pad_maximum_fusion), channel_id=1, replica_groups=mesh['seq'=4,'pair'=4,'dp'=2] {'seq'}, dimensions={0}, use_global_device_ids=true | all-gather | bytes 655360 | tf_op jit(solution)/shard_map/all_gather | solution.py:81
  48.5 1.7 %fusion.50 = f32[256,256]{0,1:T(8,128)S(1)} fusion(bf16[1536,256]{1,0:T(8,128)(2,1)} %param.13, bf16[256,1536]{1,0:T(8,128)(2,1)S(1)} %copy-done.1, f32[1536]{0:T(1024)S(1)} %copy-done.6, f32[256]{0:T(256)S(1)} %add_rsqrt_fusion.1), kind=kOutput, calls=%fused_computation.97 | convolution fusion | flops 202899456 | bytes 1842176 | tf_op jit(solution)/shard_map/dot_general | solution.py:48
  50.6 0.6 multiply_reduce_fusion
  51.2 0.5 fusion
  51.7 0.6 fusion.7
  52.4 0.4 convolution_convert_fusion
  52.8 1.2 %copy.21 = bf16[256,1536]{0,1:T(8,128)(2,1)} copy(bf16[256,1536]{1,0:T(8,128)(2,1)S(1)} %convolution_convert_fusion) | data formatting | bytes 1572864
  54.0 1.3 %collective-permute-start.2 = (bf16[18,1,128]{2,1,0:T(2,128)(2,1)S(1)}, bf16[18,1,128]{2,1,0:T(2,128)(2,1)S(1)}, u32[]{:S(2)}, u32[]{:S(2)}) collective-permute-start(bf16[18,1,128]{2,1,0:T(2,128)(2,1)S(1)} %get-tuple-element.37), channel_id=1, source_target_pairs={{0,2},{2,4},{4,6},{1,3},{3,5},{5,7},{8,10},{10,12},{12,14},{9,11},... | collective-permute-start | bytes 13832 | tf_op jit(solution)/shard_map/ppermute | solution.py:15
  55.3 1.3 %collective-permute-start.3 = (bf16[18,1,128]{2,1,0:T(2,128)(2,1)S(1)}, bf16[18,1,128]{2,1,0:T(2,128)(2,1)S(1)}, u32[]{:S(2)}, u32[]{:S(2)}) collective-permute-start(bf16[18,1,128]{2,1,0:T(2,128)(2,1)S(1)} %get-tuple-element.38), channel_id=1, source_target_pairs={{2,0},{4,2},{6,4},{3,1},{5,3},{7,5},{10,8},{12,10},{14,12},{11,9},... | collective-permute-start | bytes 13832 | tf_op jit(solution)/shard_map/ppermute | solution.py:18
  56.8 3.3 %collective-permute-done.3 = bf16[18,1,128]{2,1,0:T(2,128)(2,1)S(1)} collective-permute-done((bf16[18,1,128]{2,1,0:T(2,128)(2,1)S(1)}, bf16[18,1,128]{2,1,0:T(2,128)(2,1)S(1)}, u32[]{:S(2)}, u32[]{:S(2)}) %collective-permute-start.3) | collective-permute-done | bytes 4640 | tf_op jit(solution)/shard_map/ppermute | solution.py:18
  61.5 0.7 add_convert_fusion.2
  62.1 14.8 %reduce-scatter.4.cloned.1.call-done = bf16[384,256]{1,0:T(8,128)(2,1)} async-done(((bf16[1536,256]{1,0:T(8,128)(2,1)}), bf16[384,256]{1,0:T(8,128)(2,1)}) %reduce-scatter.4.cloned.1.call-update) | async-done | bytes 196624
  76.9 1.1 %copy.22 = bf16[256,384]{1,0:T(8,128)(2,1)S(1)} copy(bf16[256,384]{0,1:T(8,128)(2,1)} %bitcast.103) | data formatting | bytes 393216
  78.0 0.7 add_convert_fusion
  (55 shorter events, 2.4 us)
Async XLA Ops:
  7.2 45.2 %copy-start = (bf16[256,1536]{1,0:T(8,128)(2,1)S(1)}, bf16[256,1536]{1,0:T(8,128)(2,1)}, u32[]{:S(2)}) copy-start(bf16[256,1536]{1,0:T(8,128)(2,1)} %param.16) | copy-start | bytes 2359300
  7.2 24.6 %copy-start.1 = (bf16[256,1536]{1,0:T(8,128)(2,1)S(1)}, bf16[256,1536]{1,0:T(8,128)(2,1)}, u32[]{:S(2)}) copy-start(bf16[256,1536]{1,0:T(8,128)(2,1)} %param.11) | copy-start | bytes 2359300
  7.2 24.6 %copy-start.6 = (f32[1536]{0:T(1024)S(1)}, f32[1536]{0:T(1024)}, u32[]{:S(2)}) copy-start(f32[1536]{0:T(1024)} %param.12) | copy-start | bytes 18436
  7.2 3.3 %copy-start.4 = (bf16[1536,128]{1,0:T(8,128)(2,1)S(1)}, bf16[1536,128]{1,0:T(8,128)(2,1)}, u32[]{:S(2)}) copy-start(bf16[1536,128]{1,0:T(8,128)(2,1)} %param.19) | copy-start | bytes 1179652
  7.2 18.3 %copy-start.3 = (bf16[1536,128]{1,0:T(8,128)(2,1)S(1)}, bf16[1536,128]{1,0:T(8,128)(2,1)}, u32[]{:S(2)}) copy-start(bf16[1536,128]{1,0:T(8,128)(2,1)} %param.18) | copy-start | bytes 1179652
  7.2 18.4 %copy-start.2 = (bf16[16,16,128]{2,1,0:T(8,128)(2,1)S(1)}, bf16[16,16,128]{2,1,0:T(8,128)(2,1)}, u32[]{:S(2)}) copy-start(bf16[16,16,128]{2,1,0:T(8,128)(2,1)} %param.17) | copy-start | bytes 196612
  7.2 18.6 %copy-start.7 = (f32[128]{0:T(128)S(1)}, f32[128]{0:T(128)}, u32[]{:S(2)}) copy-start(f32[128]{0:T(128)} %param.20) | copy-start | bytes 1540
  7.2 24.6 %copy-start.8 = (bf16[1536,128]{1,0:T(8,128)(2,1)S(1)}, bf16[1536,128]{1,0:T(8,128)(2,1)}, u32[]{:S(2)}) copy-start(bf16[1536,128]{1,0:T(8,128)(2,1)} %param.15) | copy-start | bytes 1179652
  7.3 69.7 %reduce-scatter.4.cloned.1.call-start = ((), (), s32[]{:S(2)}) async-start(), calls=%async_computation.1 | async-start | bytes 983040
  10.5 21.8 %copy-start.9 = (bf16[1536,128]{1,0:T(8,128)(2,1)S(1)}, bf16[1536,128]{1,0:T(8,128)(2,1)}, u32[]{:S(2)}) copy-start(bf16[1536,128]{1,0:T(8,128)(2,1)} %param.14) | copy-start | bytes 1179652
  25.9 28.0 %collective-permute-start.1 = (bf16[1,16,128]{2,1,0:T(8,128)(2,1)S(1)}, bf16[1,16,128]{2,1,0:T(8,128)(2,1)S(1)}, u32[]{:S(2)}, u32[]{:S(2)}) collective-permute-start(bf16[1,16,128]{2,1,0:T(8,128)(2,1)S(1)} %get-tuple-element.42), channel_id=1, source_target_pairs={{8,0},{16,8},{24,16},{9,1},{17,9},{25,17},{10,2},{18,10},{26,18},{... | collective-permute-start | bytes 12296 | tf_op jit(solution)/shard_map/ppermute | solution.py:18
  27.2 26.7 %collective-permute-start = (bf16[1,16,128]{2,1,0:T(8,128)(2,1)S(1)}, bf16[1,16,128]{2,1,0:T(8,128)(2,1)S(1)}, u32[]{:S(2)}, u32[]{:S(2)}) collective-permute-start(bf16[1,16,128]{2,1,0:T(8,128)(2,1)S(1)} %get-tuple-element.41), channel_id=1, source_target_pairs={{0,8},{8,16},{16,24},{1,9},{9,17},{17,25},{2,10},{10,18},{18,26},{... | collective-permute-start | bytes 12296 | tf_op jit(solution)/shard_map/ppermute | solution.py:15
  52.8 3.9 %copy-start.5 = (bf16[3,3,128,128]{3,2,1,0:T(8,128)(2,1)S(1)}, bf16[3,3,128,128]{3,2,1,0:T(8,128)(2,1)}, u32[]{:S(2)}) copy-start(bf16[3,3,128,128]{3,2,1,0:T(8,128)(2,1)} %param.21) | copy-start | bytes 884740
  54.0 2.8 %collective-permute-start.2 = (bf16[18,1,128]{2,1,0:T(2,128)(2,1)S(1)}, bf16[18,1,128]{2,1,0:T(2,128)(2,1)S(1)}, u32[]{:S(2)}, u32[]{:S(2)}) collective-permute-start(bf16[18,1,128]{2,1,0:T(2,128)(2,1)S(1)} %get-tuple-element.37), channel_id=1, source_target_pairs={{0,2},{2,4},{4,6},{1,3},{3,5},{5,7},{8,10},{10,12},{12,14},{9,11},... | collective-permute-start | bytes 13832 | tf_op jit(solution)/shard_map/ppermute | solution.py:15
  55.3 4.8 %collective-permute-start.3 = (bf16[18,1,128]{2,1,0:T(2,128)(2,1)S(1)}, bf16[18,1,128]{2,1,0:T(2,128)(2,1)S(1)}, u32[]{:S(2)}, u32[]{:S(2)}) collective-permute-start(bf16[18,1,128]{2,1,0:T(2,128)(2,1)S(1)} %get-tuple-element.38), channel_id=1, source_target_pairs={{2,0},{4,2},{6,4},{3,1},{5,3},{7,5},{10,8},{12,10},{14,12},{11,9},... | collective-permute-start | bytes 13832 | tf_op jit(solution)/shard_map/ppermute | solution.py:18
Sparse Core Ops, SparseCore 0:
  54.1 22.8 reduce-scatter.3
